TPU v7x, 32 devices: a whole 2x2x4 slice. The times are simulated.
32 devices in a mesh: groups: 2 (over y), seq: 4 (over z), exp: 4 (over x, core).
Axes of the slice: x: 2, y: 2, z: 4, core: 2. Of those that a mesh axis runs over, the one named last changes fastest.
Arguments:
- residual: bfloat16 [1024, 6144], P(('groups', 'seq'), 'exp'), parts along dimension 0, may hold values from -6 to 6
- query_rows: bfloat16 [1024, 6144], P(('groups', 'seq'), 'exp'), parts along dimension 0, may hold values from -6 to 6
- key_rows: bfloat16 [1024, 6144], P(('groups', 'seq'), 'exp'), parts along dimension 0, may hold values from -6 to 6
- value_rows: bfloat16 [1024, 6144], P(('groups', 'seq'), 'exp'), parts along dimension 0, may hold values from -6 to 6
- log_decay: float32 [1024, 48], P(('groups', 'seq'), 'exp'), parts along dimension 0, may hold values from -0.8 to 0
- attn_gain: float32 [6144], P('exp'), may hold values from 0.1 to 1.9
- norm_gain: float32 [6144], P('exp'), may hold values from 0.1 to 1.9
- router: bfloat16 [6144, 32], P('exp'), may hold values from -0.3125 to 0.3125
- expert_ids: int32 [1024, 2], P(('groups', 'seq')), parts along dimension 0, may hold values from 0 to 31, all different within a row
- priority: int32 [8, 128], P(('groups', 'seq')), parts along dimension 0, may hold values from 0 to 127, each once within a row
- gate_weight: bfloat16 [4, 6144, 4608], P('exp', None, 'seq'), may hold values from -0.078125 to 0.078125
- up_weight: bfloat16 [4, 6144, 4608], P('exp', None, 'seq'), may hold values from -0.078125 to 0.078125
- down_weight: bfloat16 [4, 4608, 6144], P('exp', None, 'seq'), may hold values from -0.125 to 0.125
Outputs:
- layer_out: bfloat16 [1024, 6144], P(('groups', 'seq'), 'exp'), parts along dimension 0
There are 2 independent parts, one for each index of `groups`. A program takes and returns all parts, laid end to end along the dimension named above; an argument that names none is the same for every part. Nothing has to cross between parts.
Inputs may be any that keep to these rules, and one draw needn't show every extreme that they name: `expert_ids`: each row names two different experts; ids of 4 or more name experts whose weights are not given. `priority`: each row holds every number from 0 to 127 once.
All inputs are finite; a program needn't handle non-finite values.
Results may differ from a plain program's by a relative error of at most 0.0047.
Values may be sent and summed in bfloat16 or wider, within the bound.
A program may use at most 128 MiB of HBM per device.

v0:
```python
import functools

import jax
import jax.numpy as jnp
from jax import lax
from jax.experimental import pallas as pl
from jax.experimental.pallas import tpu as pltpu
from jax.sharding import PartitionSpec as P

D = 6144
HEAD = 128
EXPERTS = 32
CAP = 8


def link_states(earlier, later):
    return (earlier[0] * later[0], later[0] * earlier[1] + later[1])


def plain_body(
    residual,
    query_rows,
    key_rows,
    value_rows,
    log_decay,
    attn_gain,
    norm_gain,
    router,
    expert_ids,
    priority,
    gate_weight,
    up_weight,
    down_weight,
):
    rows = residual.shape[0]
    width = residual.shape[1]
    heads = width // HEAD
    held = lax.axis_size("exp")
    queries = query_rows.reshape(rows, heads, HEAD)
    keys_local = key_rows.reshape(rows, heads, HEAD)
    values = value_rows.reshape(rows, heads, HEAD)
    cumulative = jnp.cumsum(log_decay, axis=0)
    scores = jnp.einsum("thd,shd->hts", queries, keys_local, preferred_element_type=jnp.float32)
    causal = (jnp.arange(rows)[:, None] >= jnp.arange(rows)[None, :])[None]
    spread = cumulative.T[:, :, None] - cumulative.T[:, None, :]
    weights = jnp.where(causal, scores * jnp.exp(jnp.where(causal, spread, 0.0)), 0.0).astype(
        jnp.bfloat16
    )
    local_part = jnp.einsum("hts,shd->thd", weights, values, preferred_element_type=jnp.float32)
    to_end = jnp.exp(cumulative[-1][None, :] - cumulative)
    keyed = (keys_local.astype(jnp.float32) * to_end[:, :, None]).astype(jnp.bfloat16)
    block_state = jnp.einsum("thd,the->hde", keyed, values, preferred_element_type=jnp.float32)
    block_decay = jnp.exp(cumulative[-1])
    seq_count = lax.axis_size("seq")
    share_size = block_state.size // seq_count
    flat_state = block_state.reshape(seq_count, share_size)
    tiled_decay = jnp.broadcast_to(block_decay[None, :], (seq_count, heads))
    arrived_state, arrived_decay = (
        lax.all_to_all(flat_state, "seq", split_axis=0, concat_axis=0, tiled=True),
        lax.all_to_all(tiled_decay, "seq", split_axis=0, concat_axis=0, tiled=True),
    )
    position = lax.axis_index("seq") * share_size + jnp.arange(share_size, dtype=jnp.int32)
    owner_head = position // (HEAD * HEAD)
    selector = jnp.where(
        owner_head[None, :] == jnp.arange(heads, dtype=jnp.int32)[:, None], 1.0, 0.0
    ).astype(jnp.float32)
    element_decay = jnp.dot(arrived_decay, selector, precision=lax.Precision.HIGHEST)
    inclusive = lax.associative_scan(link_states, (element_decay, arrived_state), axis=0)[1]
    exclusive = jnp.concatenate([jnp.zeros((1, share_size), jnp.float32), inclusive[:-1]], axis=0)
    returned_prefix = lax.all_to_all(exclusive, "seq", split_axis=0, concat_axis=0, tiled=True)
    prior_state = returned_prefix.reshape(block_state.shape)
    inter = jnp.einsum(
        "thd,hde->the", queries.astype(jnp.float32), prior_state, precision=lax.Precision.HIGHEST
    )
    attended = local_part + jnp.exp(cumulative)[:, :, None] * inter
    normed = attended * lax.rsqrt(jnp.mean(attended * attended, axis=-1, keepdims=True) + 1e-06)
    normed = normed * attn_gain.reshape(heads, HEAD)
    mixed = (residual.astype(jnp.float32) + normed.reshape(rows, width)).astype(jnp.bfloat16)
    mixed_f = mixed.astype(jnp.float32)
    gained = mixed_f * norm_gain
    router_f = router.astype(jnp.float32)
    squares = lax.psum(jnp.sum(mixed_f * mixed_f, axis=1), "exp")
    inverse = lax.rsqrt(squares / D + 1e-06)
    scaled = gained * inverse[:, None]
    logits = lax.psum(jnp.dot(scaled, router_f, precision=lax.Precision.HIGHEST), "exp")
    tokens_in = scaled.astype(jnp.bfloat16)
    probs = jax.nn.sigmoid(logits)
    chosen = expert_ids[:, :, None] == jnp.arange(EXPERTS, dtype=jnp.int32)[None, None, :]
    selected = jnp.sum(jnp.where(chosen, probs[:, None, :], 0.0), axis=-1)
    gates = selected / jnp.sum(selected, axis=-1, keepdims=True)
    is_held = expert_ids[:, :, None] == jnp.arange(held, dtype=jnp.int32)[None, None, :]
    member = jnp.where(jnp.any(is_held, axis=1), 1.0, 0.0).astype(jnp.float32)
    gate_held = jnp.sum(jnp.where(is_held, gates[:, :, None], 0.0), axis=1)
    order = priority[0]
    earlier = jnp.where(order[None, :] < order[:, None], 1.0, 0.0).astype(jnp.bfloat16)
    rank = jnp.dot(earlier, member.astype(jnp.bfloat16), preferred_element_type=jnp.float32)
    kept = (member > 0.5) & (rank < CAP)
    slot_ids = jnp.arange(CAP).astype(jnp.float32)
    place = kept.T[:, None, :] & (rank.T[:, None, :] == slot_ids[None, :, None])
    place_f = jnp.where(place, 1.0, 0.0).astype(jnp.float32)
    buffer = jnp.einsum(
        "ect,td->ecd", place_f.astype(jnp.bfloat16), tokens_in, preferred_element_type=jnp.float32
    ).astype(jnp.bfloat16)
    arrived = lax.all_to_all(buffer, "exp", split_axis=0, concat_axis=2, tiled=True)[0]
    gathered = lax.all_gather(arrived, "seq", axis=0, tiled=True)
    gate = jnp.dot(gathered, gate_weight[0], preferred_element_type=jnp.float32)
    up = jnp.dot(gathered, up_weight[0], preferred_element_type=jnp.float32)
    hidden = (jax.nn.silu(gate) * up).astype(jnp.bfloat16)
    weight_rows = down_weight[0]
    summed = jnp.dot(
        lax.all_gather(hidden, "seq", axis=1, tiled=True),
        weight_rows,
        preferred_element_type=jnp.float32,
    )
    expert_out = summed.astype(jnp.bfloat16)
    returned = lax.all_to_all(expert_out, "seq", split_axis=0, concat_axis=1, tiled=True)
    regrouped = lax.all_to_all(returned[None], "exp", split_axis=2, concat_axis=0, tiled=True)
    weighted = place_f * gate_held.T[:, None, :]
    combined = jnp.einsum(
        "ect,ecd->td", weighted, regrouped.astype(jnp.float32), precision=lax.Precision.HIGHEST
    )
    return (mixed_f + combined).astype(jnp.bfloat16)


MESH = pl.DeviceIdType.MESH
F32 = jnp.float32
BF16 = jnp.bfloat16
WEIGHT_CUTS = 2


def layer_kernel(
    ns,
    nx,
    group,
    parts,
    residual,
    query,
    key,
    value,
    log_decay,
    attn_gain,
    norm_gain,
    router,
    ids,
    priority,
    gate_hbm,
    up_hbm,
    down_hbm,
    out,
    weights_in,
    weights_down,
    padded,
    cum_rows,
    mixed,
    states,
    chain_out,
    chain_in,
    sums_out,
    sums_in,
    slots_out,
    slots_in,
    inverse_out,
    inverse_in,
    total_in,
    hidden_all,
    total_out,
    back_out,
    back_in,
    chunks,
    weight_sems,
    down_sems,
    chain_sems,
    sums_send,
    sums_recv,
    slots_send,
    slots_recv,
    inverse_send,
    inverse_recv,
    hidden_send,
    hidden_recv,
    back_send,
    back_recv,
):
    rows, width = residual.shape
    heads = width // HEAD
    half = width // 2
    depth = weights_in.shape[0]
    ff = gate_hbm.shape[2]
    span = ff // parts
    s = lax.axis_index("seq")
    x = lax.axis_index("exp")

    barrier = pltpu.get_barrier_semaphore()
    peers = [(a, b) for a in range(ns) for b in range(nx) if (a, b) != (0, 0)]

    def peer(a, b):
        return {"seq": lax.rem(s + a, ns), "exp": lax.rem(x + b, nx)}

    for a, b in peers:
        pl.semaphore_signal(barrier, inc=1, device_id=peer(a, b), device_id_type=MESH)

    weight_copies = []
    cut = depth // WEIGHT_CUTS
    for i in range(WEIGHT_CUTS):
        at = pl.ds(i * cut, cut)
        for p in range(parts):
            for j, source in enumerate((gate_hbm, up_hbm)):
                weight_copies.append(
                    pltpu.make_async_copy(
                        source.at[0, at, pl.ds(p * span, span)],
                        weights_in.at[at, pl.ds((2 * p + j) * span, span)],
                        weight_sems.at[j * parts + p, i],
                    )
                )
    down_copies = []
    for p in range(parts):
        for i in range(ns):
            down_copies.append(
                pltpu.make_async_copy(
                    down_hbm.at[0, pl.ds(i * ff + p * span, span), :],
                    weights_down.at[pl.ds((p * ns + i) * span, span), :],
                    down_sems.at[p, i],
                )
            )
    for copy in weight_copies + down_copies:
        copy.start()

    row_at = lax.broadcasted_iota(jnp.int32, (rows, rows), 0)
    lane_at = lax.broadcasted_iota(jnp.int32, (rows, rows), 1)
    id_rows = [ids[i : i + 1, :].astype(F32) for i in range(2)]
    order = jnp.broadcast_to(priority[...].astype(F32), (rows, rows))
    earlier = jnp.where(order.T < order, 1.0, 0.0).astype(BF16)
    expert_rows = -(-nx // 8) * 8
    expert_at = lax.broadcasted_iota(jnp.int32, (expert_rows, rows), 0).astype(F32)
    member = jnp.where((id_rows[0] == expert_at) | (id_rows[1] == expert_at), 1.0, 0.0)
    rank = jnp.dot(member.astype(BF16), earlier, preferred_element_type=F32)
    slot_at = lax.broadcasted_iota(jnp.int32, (CAP, rows), 0).astype(F32)
    rank = jnp.where(member > 0.5, rank, -1.0)
    place = [jnp.where(rank[e : e + 1, :] == slot_at, 1.0, 0.0) for e in range(nx)]
    place_all = jnp.concatenate(place, axis=0)

    padded[...] = jnp.zeros_like(padded)
    padded[:heads, :] = log_decay[...]
    upper = jnp.where(row_at <= lane_at, 1.0, 0.0).astype(F32)
    cumulative = jnp.dot(
        padded[...], upper, precision=lax.Precision.HIGHEST, preferred_element_type=F32
    )
    cum_rows[...] = cumulative
    padded[...] = cumulative.T

    @pl.when(s == 0)
    def _():
        chain_in[...] = jnp.zeros_like(chain_in)

    pl.semaphore_wait(barrier, len(peers))

    def chain_copy(i):
        return pltpu.make_async_remote_copy(
            src_ref=chain_out.at[i],
            dst_ref=chain_in.at[i],
            send_sem=chain_sems.at[0, i],
            recv_sem=chain_sems.at[1, i],
            device_id={"seq": lax.rem(s + 1, ns)},
            device_id_type=MESH,
        )

    cluster = 2 * group
    for first in range(0, heads, cluster):
        for head in range(first, first + cluster):
            at = slice(head * HEAD, (head + 1) * HEAD)
            col = padded[:, head : head + 1]
            to_end = jnp.exp(col[rows - 1 : rows, :] - col)
            keyed = (key[:, at].astype(F32) * to_end).astype(BF16)
            state = lax.dot_general(
                keyed, value[:, at], (((0,), (0,)), ((), ())), preferred_element_type=F32
            )
            states[head] = state
            chain_out[head] = state.astype(BF16)

        @pl.when(s == 0)
        def _():
            for head in range(first, first + cluster):
                chain_copy(head).start()

    causal = row_at >= lane_at

    def attend(i, carry):
        cols = []
        for g in range(group):
            head = i * group + g
            cols.append(
                jnp.sum(jnp.where(lane_at == head, padded[...], 0.0), axis=1, keepdims=True)
            )

        @pl.when(s > 0)
        def _():
            for g in range(group):
                head = i * group + g
                chain_copy(head).wait_recv()

                @pl.when(s < ns - 1)
                def _():
                    decay = jnp.exp(cols[g][rows - 1 : rows, :])
                    prior = chain_in[head].astype(F32)
                    chain_out[head] = (decay * prior + states[head]).astype(BF16)
                    chain_copy(head).start()

        for g in range(group):
            head = i * group + g
            at = pl.ds(pl.multiple_of(head * HEAD, HEAD), HEAD)
            col, row = cols[g], cum_rows[pl.ds(head, 1), :]
            q, k, v = query[:, at], key[:, at], value[:, at]
            scores = lax.dot_general(q, k, (((1,), (1,)), ((), ())), preferred_element_type=F32)
            spread = jnp.where(causal, col - row, 0.0)
            weights = jnp.where(causal, scores * jnp.exp(spread), 0.0).astype(BF16)
            local = jnp.dot(weights, v, preferred_element_type=F32)
            inter = jnp.dot(q, chain_in[head], preferred_element_type=F32)
            attended = local + jnp.exp(col) * inter
            mean = jnp.sum(attended * attended, axis=1, keepdims=True) / HEAD
            normed = attended * lax.rsqrt(mean + 1e-06) * attn_gain[pl.ds(head, 1), :]
            mixed[:, at] = (residual[:, at].astype(F32) + normed).astype(BF16)
        return carry

    def slots_copy(m, a, b):
        return pltpu.make_async_remote_copy(
            src_ref=slots_out.at[m, lax.rem(x + b, nx)],
            dst_ref=slots_in.at[m, s, x],
            send_sem=slots_send.at[m, a, b],
            recv_sem=slots_recv.at[m, s, x],
            device_id=peer(a, b),
            device_id_type=MESH,
        )

    def slots_arrive(m, block, source):
        return pltpu.make_async_remote_copy(
            src_ref=slots_out.at[m, 0],
            dst_ref=slots_in.at[m, block, source],
            send_sem=slots_send.at[m, 0, 0],
            recv_sem=slots_recv.at[m, block, source],
            device_id=peer(1, 1),
            device_id_type=MESH,
        )

    place_b = place_all.astype(BF16)
    steps = heads // group // 2
    heads_half = heads // 2
    quarter = half // 2
    logits = jnp.zeros((rows, router.shape[0]), F32)
    squares = jnp.zeros((rows, 1), F32)
    for m in range(2):
        lax.fori_loop(m * steps, (m + 1) * steps, attend, 0)
        gained = []
        for head in range(m * heads_half, (m + 1) * heads_half):
            mixed_f = mixed[:, head * HEAD : (head + 1) * HEAD].astype(F32)
            squares = squares + jnp.sum(mixed_f * mixed_f, axis=1, keepdims=True)
            gained.append(mixed_f * norm_gain[head : head + 1, :])
        gained = jnp.concatenate(gained, axis=1)
        tokens = gained.astype(BF16)
        picked = jnp.dot(place_b, tokens, preferred_element_type=F32)
        for e in range(nx):
            at = slice(e * CAP, (e + 1) * CAP)
            slots_out[m, e] = jnp.concatenate(
                [picked[at, :quarter], picked[at, quarter:]], axis=0
            ).astype(BF16)
        slots_in[m, s, x] = slots_out[m, x]
        for a, b in peers:
            slots_copy(m, a, b).start()
        rest = (gained - tokens.astype(F32)).astype(BF16)
        router_half = router[:, m * half : (m + 1) * half]
        for part in (tokens, rest):
            logits = logits + lax.dot_general(
                part, router_half, (((1,), (1,)), ((), ())), preferred_element_type=F32
            )

    padded[...] = jnp.zeros_like(padded)
    padded[:, : router.shape[0]] = logits
    logits_t = padded[...].T
    expert_row = row_at.astype(F32)
    chosen = [
        jnp.sum(jnp.where(expert_row == r, logits_t, 0.0), axis=0, keepdims=True) for r in id_rows
    ]
    squares_t = jnp.broadcast_to(squares, (rows, rows)).T[0:1, :]
    sums = jnp.concatenate([chosen[0], chosen[1], squares_t] + [squares_t] * 5, axis=0)
    sums_out[...] = sums
    sums_in[x] = sums

    def sums_copy(b):
        return pltpu.make_async_remote_copy(
            src_ref=sums_out,
            dst_ref=sums_in.at[x],
            send_sem=sums_send.at[b],
            recv_sem=sums_recv.at[x],
            device_id=peer(0, b),
            device_id_type=MESH,
        )

    def sums_arrive(b):
        source = lax.rem(x + b, nx)
        return pltpu.make_async_remote_copy(
            src_ref=sums_out,
            dst_ref=sums_in.at[source],
            send_sem=sums_send.at[b],
            recv_sem=sums_recv.at[source],
            device_id=peer(0, b),
            device_id_type=MESH,
        )

    for b in range(1, nx):
        sums_copy(b).start()

    def slots_wait(m):
        for a, b in peers:
            slots_arrive(m, lax.rem(s + a, ns), lax.rem(x + b, nx)).wait_recv()

    def chunk_of(m, source):
        arrived = [slots_in[m, i, source].astype(F32) for i in range(ns)]
        return jnp.concatenate(
            [
                jnp.concatenate([r[h * CAP : (h + 1) * CAP] for r in arrived], axis=0)
                for h in range(2)
            ],
            axis=1,
        ).astype(BF16)

    def product_of(m, held, at):
        product = None
        for source in range(nx):
            start = source * width + m * half
            term = jnp.dot(
                held[source], weights_in[start : start + half, at], preferred_element_type=F32
            )
            product = term if product is None else product + term
        return product

    slots_wait(0)
    for copy in weight_copies:
        copy.wait()
    held = [chunk_of(0, source) for source in range(nx)]
    for p in range(parts):
        at = slice(2 * p * span, 2 * (p + 1) * span)
        total_in[:, at] = product_of(0, held, at)

    for b in range(1, nx):
        sums_arrive(b).wait_recv()
    added = sums_in[0]
    for b in range(1, nx):
        added = added + sums_in[b]
    inverse = lax.rsqrt(added[2:3, :] / (width * nx) + 1e-06)
    slot_inverse = jnp.sum(place_all * inverse, axis=1, keepdims=True)
    slot_inverse = jnp.broadcast_to(slot_inverse, place_all.shape)
    for e in range(nx):
        inverse_out[e] = slot_inverse[e * CAP : (e + 1) * CAP, :]
    inverse_in[s] = inverse_out[x]

    def inverse_copy(a):
        return pltpu.make_async_remote_copy(
            src_ref=inverse_out.at[x],
            dst_ref=inverse_in.at[s],
            send_sem=inverse_send.at[a],
            recv_sem=inverse_recv.at[s],
            device_id=peer(a, 0),
            device_id_type=MESH,
        )

    def inverse_arrive(a):
        source = lax.rem(s + a, ns)
        return pltpu.make_async_remote_copy(
            src_ref=inverse_out.at[x],
            dst_ref=inverse_in.at[source],
            send_sem=inverse_send.at[a],
            recv_sem=inverse_recv.at[source],
            device_id=peer(a, 0),
            device_id_type=MESH,
        )

    for a in range(1, ns):
        inverse_copy(a).start()

    slots_wait(1)
    for source in range(nx):
        chunks[source] = chunk_of(1, source)
    for a in range(1, ns):
        inverse_arrive(a).wait_recv()
    scale = jnp.concatenate([inverse_in[i] for i in range(ns)], axis=0)[:, :1]

    def hidden_copy(p, a):
        return pltpu.make_async_remote_copy(
            src_ref=hidden_all.at[s, p],
            dst_ref=hidden_all.at[s, p],
            send_sem=hidden_send.at[p, a],
            recv_sem=hidden_recv.at[p, s],
            device_id=peer(a, 0),
            device_id_type=MESH,
        )

    def hidden_arrive(p, a):
        source = lax.rem(s + a, ns)
        return pltpu.make_async_remote_copy(
            src_ref=hidden_all.at[s, p],
            dst_ref=hidden_all.at[source, p],
            send_sem=hidden_send.at[p, a],
            recv_sem=hidden_recv.at[p, source],
            device_id=peer(a, 0),
            device_id_type=MESH,
        )

    for p in range(parts):
        at = slice(2 * p * span, 2 * (p + 1) * span)
        product = (total_in[:, at] + product_of(1, chunks, at)) * scale
        hidden_all[s, p] = (jax.nn.silu(product[:, :span]) * product[:, span:]).astype(BF16)
        for a in range(1, ns):
            hidden_copy(p, a).start()

    probs = [jax.nn.sigmoid(added[i : i + 1, :] * inverse) for i in range(2)]
    gates = [r / (probs[0] + probs[1]) for r in probs]
    weighted = jnp.concatenate(
        [
            place[e]
            * (
                jnp.where(id_rows[0] == e, gates[0], 0.0)
                + jnp.where(id_rows[1] == e, gates[1], 0.0)
            )
            for e in range(nx)
        ],
        axis=0,
    )
    slots = nx * CAP
    padded[...] = jnp.zeros_like(padded)
    padded[:slots, :] = weighted
    weighted = padded[...].T[:, :slots]
    weighted_high = weighted.astype(BF16)
    weighted_low = (weighted - weighted_high.astype(F32)).astype(BF16)

    for copy in down_copies:
        copy.wait()

    def down_product(p, at):
        hidden = jnp.concatenate([hidden_all[i, p] for i in range(ns)], axis=1)
        return jnp.dot(
            hidden,
            weights_down[p * ns * span : (p + 1) * ns * span, at],
            preferred_element_type=F32,
        )

    def back_copy(h, block):
        return pltpu.make_async_remote_copy(
            src_ref=back_out.at[h, block],
            dst_ref=back_in.at[h, x],
            send_sem=back_send.at[h, block],
            recv_sem=back_recv.at[h, x],
            device_id={"seq": block, "exp": s},
            device_id_type=MESH,
        )

    def back_arrive(h, e):
        return pltpu.make_async_remote_copy(
            src_ref=back_out.at[h, 0],
            dst_ref=back_in.at[h, e],
            send_sem=back_send.at[h, 0],
            recv_sem=back_recv.at[h, e],
            device_id={"seq": x, "exp": e},
            device_id_type=MESH,
        )

    for p in range(parts):
        for a in range(1, ns):
            hidden_arrive(p, a).wait_recv()
        if p < parts - 1:
            product = down_product(p, slice(0, width))
            total_out[...] = product if p == 0 else total_out[...] + product
    for h in range(2):
        at = slice(h * half, (h + 1) * half)
        total = down_product(parts - 1, at)
        if parts > 1:
            total = total + total_out[:, at]
        for b in range(ns):
            of = slice(b * CAP, (b + 1) * CAP)
            back_out[h, b] = jnp.concatenate(
                [total[of, :quarter], total[of, quarter:]], axis=0
            ).astype(BF16)
        for a in range(1, ns):
            back_copy(h, lax.rem(s + a, ns)).start()

        @pl.when(x != s)
        def _():
            back_copy(h, s).start()

        @pl.when(x == s)
        def _():
            back_in[h, x] = back_out[h, s]

    for h in range(2):
        for b in range(1, nx):
            back_arrive(h, lax.rem(x + b, nx)).wait_recv()

        @pl.when(x != s)
        def _():
            back_arrive(h, x).wait_recv()

        returned = [back_in[h, e].astype(F32) for e in range(nx)]
        expert_out = jnp.concatenate(
            [
                jnp.concatenate([r[j * CAP : (j + 1) * CAP] for r in returned], axis=0)
                for j in range(2)
            ],
            axis=1,
        ).astype(BF16)
        combined = jnp.dot(weighted_high, expert_out, preferred_element_type=F32) + jnp.dot(
            weighted_low, expert_out, preferred_element_type=F32
        )
        at = slice(h * half, (h + 1) * half)
        out[:, at] = (mixed[:, at].astype(F32) + combined).astype(BF16)

    @pl.when(s < ns - 1)
    def _():
        for head in range(heads):
            chain_copy(head).wait_send()

    for m in range(2):
        for a, b in peers:
            slots_copy(m, a, b).wait_send()
    for b in range(1, nx):
        sums_copy(b).wait_send()
    for a in range(1, ns):
        inverse_copy(a).wait_send()
        for p in range(parts):
            hidden_copy(p, a).wait_send()
    for h in range(2):
        for a in range(1, ns):
            back_copy(h, lax.rem(s + a, ns)).wait_send()

        @pl.when(x != s)
        def _():
            back_copy(h, s).wait_send()


def fused_body(
    residual,
    query_rows,
    key_rows,
    value_rows,
    log_decay,
    attn_gain,
    norm_gain,
    router,
    expert_ids,
    priority,
    gate_weight,
    up_weight,
    down_weight,
):
    ns, nx = lax.axis_size("seq"), lax.axis_size("exp")
    rows, width = residual.shape
    heads = width // HEAD
    group = 2 if heads % 4 == 0 else 1
    depth, ff = gate_weight.shape[1:]
    half = width // 2
    parts = next(n for n in (3, 2, 1) if ff % (n * HEAD) == 0)
    dma = pltpu.SemaphoreType.DMA
    in_vmem = pl.BlockSpec(memory_space=pltpu.VMEM)
    in_place = pl.BlockSpec(memory_space=pl.ANY)
    return pl.pallas_call(
        functools.partial(layer_kernel, ns, nx, group, parts),
        out_shape=jax.ShapeDtypeStruct((rows, width), BF16),
        in_specs=[in_vmem] * 10 + [in_place] * 3,
        out_specs=in_vmem,
        scratch_shapes=[
            pltpu.VMEM((depth, 2 * ff), BF16),
            pltpu.VMEM(down_weight.shape[1:], BF16),
            pltpu.VMEM((rows, rows), F32),
            pltpu.VMEM((rows, rows), F32),
            pltpu.VMEM((rows, width), BF16),
            pltpu.VMEM((heads, HEAD, HEAD), F32),
            pltpu.VMEM((heads, HEAD, HEAD), BF16),
            pltpu.VMEM((heads, HEAD, HEAD), BF16),
            pltpu.VMEM((8, rows), F32),
            pltpu.VMEM((nx, 8, rows), F32),
            pltpu.VMEM((2, nx, 2 * CAP, half // 2), BF16),
            pltpu.VMEM((2, ns, nx, 2 * CAP, half // 2), BF16),
            pltpu.VMEM((nx, CAP, rows), F32),
            pltpu.VMEM((ns, CAP, rows), F32),
            pltpu.VMEM((ns * CAP, 2 * ff), F32),
            pltpu.VMEM((ns, parts, ns * CAP, ff // parts), BF16),
            pltpu.VMEM((ns * CAP, width), F32),
            pltpu.VMEM((2, ns, 2 * CAP, half // 2), BF16),
            pltpu.VMEM((2, nx, 2 * CAP, half // 2), BF16),
            pltpu.VMEM((nx, ns * CAP, half), BF16),
            dma((2 * parts, WEIGHT_CUTS)),
            dma((parts, ns)),
            dma((2, heads)),
            dma((nx,)),
            dma((nx,)),
            dma((2, ns, nx)),
            dma((2, ns, nx)),
            dma((ns,)),
            dma((ns,)),
            dma((parts, ns)),
            dma((parts, ns)),
            dma((2, ns)),
            dma((2, nx)),
        ],
        compiler_params=pltpu.CompilerParams(
            collective_id=0, has_side_effects=True, vmem_limit_bytes=60 * 1024 * 1024
        ),
        cost_estimate=pl.CostEstimate(
            flops=6 * ns * CAP * depth * ff,
            bytes_accessed=6 * depth * ff,
            transcendentals=heads * rows * rows,
        ),
    )(
        residual,
        query_rows,
        key_rows,
        value_rows,
        log_decay.T,
        attn_gain.reshape(heads, HEAD),
        norm_gain.reshape(heads, HEAD),
        router.T,
        expert_ids.T,
        priority,
        gate_weight,
        up_weight,
        down_weight,
    )


def body(*args):
    rows, width = args[0].shape
    ff, columns = args[10].shape[2], args[12].shape[2]
    aligned = (
        rows == HEAD
        and ff % HEAD == 0
        and width % (4 * HEAD) == 0
        and columns == width
        and args[10].shape[0] == 1
        and lax.axis_size("seq") == lax.axis_size("exp")
    )
    return (fused_body if aligned else plain_body)(*args)


def solution(mesh):
    return jax.shard_map(
        body,
        mesh=mesh,
        in_specs=(
            P(("groups", "seq"), "exp"),
            P(("groups", "seq"), "exp"),
            P(("groups", "seq"), "exp"),
            P(("groups", "seq"), "exp"),
            P(("groups", "seq"), "exp"),
            P("exp"),
            P("exp"),
            P("exp", None),
            P(("groups", "seq"), None),
            P(("groups", "seq"), None),
            P("exp", None, "seq"),
            P("exp", None, "seq"),
            P("exp", None, "seq"),
        ),
        out_specs=P(("groups", "seq"), "exp"),
        check_vma=False,
    )
```

profile of v0, /device:TPU:3, one launch (start us, length us, event | category | flops | bytes accessed | tf_op | source)
XLA Modules:
  0.0 56.2 jit_solution(2652512549163368562)
XLA Ops:
  0.0 54.4 %shard_map.127 = bf16[128,1536]{1,0:T(8,128)(2,1)} custom-call(bf16[128,1536]{1,0:T(8,128)(2,1)} %residual.1, bf16[128,1536]{1,0:T(8,128)(2,1)} %query.1, bf16[128,1536]{1,0:T(8,128)(2,1)} %key.1, bf16[128,1536]{1,0:T(8,128)(2,1)} %value.1, f32[12,128]{1,0:T(8,128)} %bitcast.6, f32[12,128]{1,0:T(8,128)} %bitcast.7, f32[12,128]{1,0:T(8,128)} %bitcast.8, ...), custom_call_target="tpu_custom_call" | custom-call | flops 1358954496 | bytes 42467328 | tf_op jit(solution)/shard_map/pallas_call | solution.py:662
  54.4 1.8 %copy.15 = bf16[128,1536]{1,0:T(8,128)(2,1)} copy(bf16[128,1536]{1,0:T(8,128)(2,1)} %shard_map.127) | data formatting | bytes 786432
where the time goes:
time: 56.3 us; the launch traced here: 56.2 us
  Pallas kernels  54.4 us (97%)
  local copies, waits for them, and re-layouts  1.77 us (3%)
    pallas_call x1, Pallas kernels, fused_body(): pl.pallas_call(functools.partial(layer_kernel, ns, nx, group, parts), out...  54.4 us
    unnamed x1, local copies, waits for them, and re-layouts  1.77 us

commit v1 on v0

--- a/solution.py
+++ b/solution.py
@@ -125,7 +125,6 @@
 MESH = pl.DeviceIdType.MESH
 F32 = jnp.float32
 BF16 = jnp.bfloat16
-WEIGHT_CUTS = 2
 
 
 def layer_kernel(
@@ -147,7 +146,8 @@
     up_hbm,
     down_hbm,
     out,
-    weights_in,
+    weights_gate,
+    weights_up,
     weights_down,
     padded,
     cum_rows,
@@ -184,7 +184,6 @@
     rows, width = residual.shape
     heads = width // HEAD
     half = width // 2
-    depth = weights_in.shape[0]
     ff = gate_hbm.shape[2]
     span = ff // parts
     s = lax.axis_index("seq")
@@ -199,31 +198,34 @@
     for a, b in peers:
         pl.semaphore_signal(barrier, inc=1, device_id=peer(a, b), device_id_type=MESH)
 
-    weight_copies = []
-    cut = depth // WEIGHT_CUTS
-    for i in range(WEIGHT_CUTS):
-        at = pl.ds(i * cut, cut)
-        for p in range(parts):
-            for j, source in enumerate((gate_hbm, up_hbm)):
-                weight_copies.append(
+    weight_copies = [[], []]
+    for m in range(2):
+        for source in range(nx):
+            at = pl.ds(source * width + m * half, half)
+            weight_copies[m].append(
+                [
                     pltpu.make_async_copy(
-                        source.at[0, at, pl.ds(p * span, span)],
-                        weights_in.at[at, pl.ds((2 * p + j) * span, span)],
-                        weight_sems.at[j * parts + p, i],
-                    )
-                )
-    down_copies = []
-    for p in range(parts):
-        for i in range(ns):
-            down_copies.append(
-                pltpu.make_async_copy(
-                    down_hbm.at[0, pl.ds(i * ff + p * span, span), :],
-                    weights_down.at[pl.ds((p * ns + i) * span, span), :],
-                    down_sems.at[p, i],
-                )
+                        gate_hbm.at[0, at, :], weights_gate.at[at, :], weight_sems.at[0, m, source]
+                    ),
+                    pltpu.make_async_copy(
+                        up_hbm.at[0, at, :], weights_up.at[at, :], weight_sems.at[1, m, source]
+                    ),
+                ]
             )
-    for copy in weight_copies + down_copies:
-        copy.start()
+    down_copies = [
+        [
+            pltpu.make_async_copy(
+                down_hbm.at[0, pl.ds(i * ff + p * span, span), :],
+                weights_down.at[pl.ds((p * ns + i) * span, span), :],
+                down_sems.at[p, i],
+            )
+            for i in range(ns)
+        ]
+        for p in range(parts)
+    ]
+    for copies in weight_copies[0] + weight_copies[1] + down_copies:
+        for copy in copies:
+            copy.start()
 
     row_at = lax.broadcasted_iota(jnp.int32, (rows, rows), 0)
     lane_at = lax.broadcasted_iota(jnp.int32, (rows, rows), 1)
@@ -422,23 +424,21 @@
             axis=1,
         ).astype(BF16)
 
-    def product_of(m, held, at):
-        product = None
-        for source in range(nx):
-            start = source * width + m * half
-            term = jnp.dot(
-                held[source], weights_in[start : start + half, at], preferred_element_type=F32
-            )
-            product = term if product is None else product + term
-        return product
+    def product_of(m, source, chunk, at):
+        start = source * width + m * half
+        return [
+            jnp.dot(chunk, w[start : start + half, at], preferred_element_type=F32)
+            for w in (weights_gate, weights_up)
+        ]
 
     slots_wait(0)
-    for copy in weight_copies:
-        copy.wait()
-    held = [chunk_of(0, source) for source in range(nx)]
-    for p in range(parts):
-        at = slice(2 * p * span, 2 * (p + 1) * span)
-        total_in[:, at] = product_of(0, held, at)
+    for source in range(nx):
+        for copy in weight_copies[0][source]:
+            copy.wait()
+        products = product_of(0, source, chunk_of(0, source), slice(0, ff))
+        for j in range(2):
+            at = slice(j * ff, (j + 1) * ff)
+            total_in[:, at] = products[j] if source == 0 else total_in[:, at] + products[j]
 
     for b in range(1, nx):
         sums_arrive(b).wait_recv()
@@ -505,9 +505,15 @@
         )
 
     for p in range(parts):
-        at = slice(2 * p * span, 2 * (p + 1) * span)
-        product = (total_in[:, at] + product_of(1, chunks, at)) * scale
-        hidden_all[s, p] = (jax.nn.silu(product[:, :span]) * product[:, span:]).astype(BF16)
+        gate = total_in[:, p * span : (p + 1) * span]
+        up = total_in[:, ff + p * span : ff + (p + 1) * span]
+        for source in range(nx):
+            if p == 0:
+                for copy in weight_copies[1][source]:
+                    copy.wait()
+            products = product_of(1, source, chunks[source], slice(p * span, (p + 1) * span))
+            gate, up = gate + products[0], up + products[1]
+        hidden_all[s, p] = (jax.nn.silu(gate * scale) * (up * scale)).astype(BF16)
         for a in range(1, ns):
             hidden_copy(p, a).start()
 
@@ -531,9 +537,6 @@
     weighted_high = weighted.astype(BF16)
     weighted_low = (weighted - weighted_high.astype(F32)).astype(BF16)
 
-    for copy in down_copies:
-        copy.wait()
-
     def down_product(p, at):
         hidden = jnp.concatenate([hidden_all[i, p] for i in range(ns)], axis=1)
         return jnp.dot(
@@ -565,6 +568,8 @@
     for p in range(parts):
         for a in range(1, ns):
             hidden_arrive(p, a).wait_recv()
+        for copy in down_copies[p]:
+            copy.wait()
         if p < parts - 1:
             product = down_product(p, slice(0, width))
             total_out[...] = product if p == 0 else total_out[...] + product
@@ -665,7 +670,8 @@
         in_specs=[in_vmem] * 10 + [in_place] * 3,
         out_specs=in_vmem,
         scratch_shapes=[
-            pltpu.VMEM((depth, 2 * ff), BF16),
+            pltpu.VMEM((depth, ff), BF16),
+            pltpu.VMEM((depth, ff), BF16),
             pltpu.VMEM(down_weight.shape[1:], BF16),
             pltpu.VMEM((rows, rows), F32),
             pltpu.VMEM((rows, rows), F32),
@@ -685,7 +691,7 @@
             pltpu.VMEM((2, ns, 2 * CAP, half // 2), BF16),
             pltpu.VMEM((2, nx, 2 * CAP, half // 2), BF16),
             pltpu.VMEM((nx, ns * CAP, half), BF16),
-            dma((2 * parts, WEIGHT_CUTS)),
+            dma((2, 2, nx)),
             dma((parts, ns)),
             dma((2, heads)),
             dma((nx,)),

time: 56.3 us -> 56 us (level)
  no operation moved by 1% of the time
where the time goes in v1:
time: 56 us; the launch traced here: 55.8 us
  Pallas kernels  54 us (96%)
  local copies, waits for them, and re-layouts  1.77 us (3%)
    pallas_call x1, Pallas kernels, fused_body(): pl.pallas_call(functools.partial(layer_kernel, ns, nx, group, parts), out...  54 us
    unnamed x1, local copies, waits for them, and re-layouts  1.77 us

profile of v1, /device:TPU:3, one launch (start us, length us, event | category | flops | bytes accessed | tf_op | source)
XLA Modules:
  0.0 55.8 jit_solution(18107539380673683462)
XLA Ops:
  0.0 54.0 %shard_map.127 = bf16[128,1536]{1,0:T(8,128)(2,1)} custom-call(bf16[128,1536]{1,0:T(8,128)(2,1)} %residual.1, bf16[128,1536]{1,0:T(8,128)(2,1)} %query.1, bf16[128,1536]{1,0:T(8,128)(2,1)} %key.1, bf16[128,1536]{1,0:T(8,128)(2,1)} %value.1, f32[12,128]{1,0:T(8,128)} %bitcast.6, f32[12,128]{1,0:T(8,128)} %bitcast.7, f32[12,128]{1,0:T(8,128)} %bitcast.8, ...), custom_call_target="tpu_custom_call" | custom-call | flops 1358954496 | bytes 42467328 | tf_op jit(solution)/shard_map/pallas_call | solution.py:667
  54.0 1.8 %copy.15 = bf16[128,1536]{1,0:T(8,128)(2,1)} copy(bf16[128,1536]{1,0:T(8,128)(2,1)} %shard_map.127) | data formatting | bytes 786432

commit v2 on v1

--- a/solution.py
+++ b/solution.py
@@ -124,6 +124,7 @@
 
 MESH = pl.DeviceIdType.MESH
 F32 = jnp.float32
+INPUTS = 10
 BF16 = jnp.bfloat16
 
 
@@ -132,22 +133,17 @@
     nx,
     group,
     parts,
-    residual,
-    query,
-    key,
-    value,
-    log_decay,
-    attn_gain,
-    norm_gain,
-    router,
-    ids,
-    priority,
-    gate_hbm,
-    up_hbm,
-    down_hbm,
+    *refs,
+):
+    arrays, refs = refs[:INPUTS], refs[INPUTS:]
+    (gate_hbm, up_hbm, down_hbm, out_hbm), refs = refs[:4], refs[4:]
+    local, refs = refs[:INPUTS], refs[INPUTS:]
+    (residual, query, key, value, log_decay, attn_gain, norm_gain, router, ids, priority) = local
+    (
     out,
-    weights_gate,
-    weights_up,
+    input_sems,
+    out_sems,
+    weights_in,
     weights_down,
     padded,
     cum_rows,
@@ -180,11 +176,11 @@
     hidden_recv,
     back_send,
     back_recv,
-):
+    ) = refs
     rows, width = residual.shape
     heads = width // HEAD
     half = width // 2
-    ff = gate_hbm.shape[2]
+    ff = gate_hbm.shape[3]
     span = ff // parts
     s = lax.axis_index("seq")
     x = lax.axis_index("exp")
@@ -198,35 +194,36 @@
     for a, b in peers:
         pl.semaphore_signal(barrier, inc=1, device_id=peer(a, b), device_id_type=MESH)
 
-    weight_copies = [[], []]
-    for m in range(2):
-        for source in range(nx):
-            at = pl.ds(source * width + m * half, half)
-            weight_copies[m].append(
-                [
-                    pltpu.make_async_copy(
-                        gate_hbm.at[0, at, :], weights_gate.at[at, :], weight_sems.at[0, m, source]
-                    ),
-                    pltpu.make_async_copy(
-                        up_hbm.at[0, at, :], weights_up.at[at, :], weight_sems.at[1, m, source]
-                    ),
-                ]
-            )
-    down_copies = [
+    input_copies = {}
+    for i in (4, 8, 9, 2, 3, 1, 0, 5, 6, 7):
+        input_copies[i] = pltpu.make_async_copy(arrays[i], local[i], input_sems.at[i])
+        input_copies[i].start()
+
+    def ready(*which):
+        for i in which:
+            input_copies[i].wait()
+
+    weight_copies = [
         [
             pltpu.make_async_copy(
-                down_hbm.at[0, pl.ds(i * ff + p * span, span), :],
-                weights_down.at[pl.ds((p * ns + i) * span, span), :],
-                down_sems.at[p, i],
+                source.at[:, m, :, pl.ds(p * span, span)],
+                weights_in.at[:, m, :, pl.ds((2 * p + j) * span, span)],
+                weight_sems.at[m, p, j],
             )
-            for i in range(ns)
+            for p in range(parts)
+            for j, source in enumerate((gate_hbm, up_hbm))
         ]
+        for m in range(2)
+    ]
+    down_copies = [
+        [pltpu.make_async_copy(down_hbm.at[:, p], weights_down.at[p], down_sems.at[p])]
         for p in range(parts)
     ]
-    for copies in weight_copies[0] + weight_copies[1] + down_copies:
+    for copies in weight_copies + down_copies:
         for copy in copies:
             copy.start()
 
+    ready(4, 8, 9)
     row_at = lax.broadcasted_iota(jnp.int32, (rows, rows), 0)
     lane_at = lax.broadcasted_iota(jnp.int32, (rows, rows), 1)
     id_rows = [ids[i : i + 1, :].astype(F32) for i in range(2)]
@@ -266,6 +263,7 @@
             device_id_type=MESH,
         )
 
+    ready(2, 3)
     cluster = 2 * group
     for first in range(0, heads, cluster):
         for head in range(first, first + cluster):
@@ -315,9 +313,9 @@
             scores = lax.dot_general(q, k, (((1,), (1,)), ((), ())), preferred_element_type=F32)
             spread = jnp.where(causal, col - row, 0.0)
             weights = jnp.where(causal, scores * jnp.exp(spread), 0.0).astype(BF16)
-            local = jnp.dot(weights, v, preferred_element_type=F32)
+            nearby = jnp.dot(weights, v, preferred_element_type=F32)
             inter = jnp.dot(q, chain_in[head], preferred_element_type=F32)
-            attended = local + jnp.exp(col) * inter
+            attended = nearby + jnp.exp(col) * inter
             mean = jnp.sum(attended * attended, axis=1, keepdims=True) / HEAD
             normed = attended * lax.rsqrt(mean + 1e-06) * attn_gain[pl.ds(head, 1), :]
             mixed[:, at] = (residual[:, at].astype(F32) + normed).astype(BF16)
@@ -343,6 +341,7 @@
             device_id_type=MESH,
         )
 
+    ready(1, 0, 5, 6, 7)
     place_b = place_all.astype(BF16)
     steps = heads // group // 2
     heads_half = heads // 2
@@ -425,20 +424,14 @@
         ).astype(BF16)
 
     def product_of(m, source, chunk, at):
-        start = source * width + m * half
-        return [
-            jnp.dot(chunk, w[start : start + half, at], preferred_element_type=F32)
-            for w in (weights_gate, weights_up)
-        ]
+        return jnp.dot(chunk, weights_in[source, m, :, at], preferred_element_type=F32)
 
     slots_wait(0)
+    for copy in weight_copies[0]:
+        copy.wait()
     for source in range(nx):
-        for copy in weight_copies[0][source]:
-            copy.wait()
-        products = product_of(0, source, chunk_of(0, source), slice(0, ff))
-        for j in range(2):
-            at = slice(j * ff, (j + 1) * ff)
-            total_in[:, at] = products[j] if source == 0 else total_in[:, at] + products[j]
+        product = product_of(0, source, chunk_of(0, source), slice(0, 2 * ff))
+        total_in[...] = product if source == 0 else total_in[...] + product
 
     for b in range(1, nx):
         sums_arrive(b).wait_recv()
@@ -504,16 +497,15 @@
             device_id_type=MESH,
         )
 
+    for copy in weight_copies[1]:
+        copy.wait()
     for p in range(parts):
-        gate = total_in[:, p * span : (p + 1) * span]
-        up = total_in[:, ff + p * span : ff + (p + 1) * span]
+        at = slice(2 * p * span, 2 * (p + 1) * span)
+        product = total_in[:, at]
         for source in range(nx):
-            if p == 0:
-                for copy in weight_copies[1][source]:
-                    copy.wait()
-            products = product_of(1, source, chunks[source], slice(p * span, (p + 1) * span))
-            gate, up = gate + products[0], up + products[1]
-        hidden_all[s, p] = (jax.nn.silu(gate * scale) * (up * scale)).astype(BF16)
+            product = product + product_of(1, source, chunks[source], at)
+        product = product * scale
+        hidden_all[s, p] = (jax.nn.silu(product[:, :span]) * product[:, span:]).astype(BF16)
         for a in range(1, ns):
             hidden_copy(p, a).start()
 
@@ -541,7 +533,7 @@
         hidden = jnp.concatenate([hidden_all[i, p] for i in range(ns)], axis=1)
         return jnp.dot(
             hidden,
-            weights_down[p * ns * span : (p + 1) * ns * span, at],
+            weights_down[p, :, :, at].reshape(ns * span, -1),
             preferred_element_type=F32,
         )
 
@@ -594,6 +586,10 @@
         def _():
             back_in[h, x] = back_out[h, s]
 
+    def out_copy(h):
+        at = pl.ds(h * half, half)
+        return pltpu.make_async_copy(out.at[:, at], out_hbm.at[:, at], out_sems.at[h])
+
     for h in range(2):
         for b in range(1, nx):
             back_arrive(h, lax.rem(x + b, nx)).wait_recv()
@@ -615,6 +611,10 @@
         )
         at = slice(h * half, (h + 1) * half)
         out[:, at] = (mixed[:, at].astype(F32) + combined).astype(BF16)
+        out_copy(h).start()
+
+    for h in range(2):
+        out_copy(h).wait()
 
     @pl.when(s < ns - 1)
     def _():
@@ -662,17 +662,31 @@
     half = width // 2
     parts = next(n for n in (3, 2, 1) if ff % (n * HEAD) == 0)
     dma = pltpu.SemaphoreType.DMA
-    in_vmem = pl.BlockSpec(memory_space=pltpu.VMEM)
+    inputs = (
+        residual,
+        query_rows,
+        key_rows,
+        value_rows,
+        log_decay.T,
+        attn_gain.reshape(heads, HEAD),
+        norm_gain.reshape(heads, HEAD),
+        router.T,
+        expert_ids.T,
+        priority,
+    )
     in_place = pl.BlockSpec(memory_space=pl.ANY)
     return pl.pallas_call(
         functools.partial(layer_kernel, ns, nx, group, parts),
         out_shape=jax.ShapeDtypeStruct((rows, width), BF16),
-        in_specs=[in_vmem] * 10 + [in_place] * 3,
-        out_specs=in_vmem,
-        scratch_shapes=[
-            pltpu.VMEM((depth, ff), BF16),
-            pltpu.VMEM((depth, ff), BF16),
-            pltpu.VMEM(down_weight.shape[1:], BF16),
+        in_specs=[in_place] * (INPUTS + 3),
+        out_specs=in_place,
+        scratch_shapes=[pltpu.VMEM(a.shape, a.dtype) for a in inputs]
+        + [
+            pltpu.VMEM((rows, width), BF16),
+            dma((INPUTS,)),
+            dma((2,)),
+            pltpu.VMEM((nx, 2, half, 2 * ff), BF16),
+            pltpu.VMEM((parts, ns, ff // parts, width), BF16),
             pltpu.VMEM((rows, rows), F32),
             pltpu.VMEM((rows, rows), F32),
             pltpu.VMEM((rows, width), BF16),
@@ -691,8 +705,8 @@
             pltpu.VMEM((2, ns, 2 * CAP, half // 2), BF16),
             pltpu.VMEM((2, nx, 2 * CAP, half // 2), BF16),
             pltpu.VMEM((nx, ns * CAP, half), BF16),
-            dma((2, 2, nx)),
-            dma((parts, ns)),
+            dma((2, parts, 2)),
+            dma((parts,)),
             dma((2, heads)),
             dma((nx,)),
             dma((nx,)),
@@ -714,19 +728,10 @@
             transcendentals=heads * rows * rows,
         ),
     )(
-        residual,
-        query_rows,
-        key_rows,
-        value_rows,
-        log_decay.T,
-        attn_gain.reshape(heads, HEAD),
-        norm_gain.reshape(heads, HEAD),
-        router.T,
-        expert_ids.T,
-        priority,
-        gate_weight,
-        up_weight,
-        down_weight,
+        *inputs,
+        gate_weight.reshape(nx, 2, half, ff),
+        up_weight.reshape(nx, 2, half, ff),
+        down_weight.reshape(ns, parts, ff // parts, width),
     )
 
 

time: 56 us -> 54.9 us (0.980)
  Pallas kernels: 54 us -> 52.9 us
    pallas_call x1, Pallas kernels: 54 us -> 52.9 us  [fused_body(): pl.pallas_call(functools.partial(layer_kernel, ns, nx, group, parts), out...]
where the time goes in v2:
time: 54.9 us; the launch traced here: 54.7 us
  Pallas kernels  52.9 us (96%)
  local copies, waits for them, and re-layouts  1.77 us (3%)
    pallas_call x1, Pallas kernels, fused_body(): pl.pallas_call(functools.partial(layer_kernel, ns, nx, group, parts), out...  52.9 us
    unnamed x1, local copies, waits for them, and re-layouts  1.77 us

profile of v2, /device:TPU:3, one launch (start us, length us, event | category | flops | bytes accessed | tf_op | source)
XLA Modules:
  0.0 54.7 jit_solution(7723619262351194647)
XLA Ops:
  0.0 52.9 %shard_map.127 = bf16[128,1536]{1,0:T(8,128)(2,1)} custom-call(bf16[128,1536]{1,0:T(8,128)(2,1)} %refs_0_.1, bf16[128,1536]{1,0:T(8,128)(2,1)} %refs_1_.1, bf16[128,1536]{1,0:T(8,128)(2,1)} %refs_2_.1, bf16[128,1536]{1,0:T(8,128)(2,1)} %refs_3_.1, f32[12,128]{1,0:T(8,128)} %bitcast.12, f32[12,128]{1,0:T(8,128)} %bitcast.13, f32[12,128]{1,0:T(8,128)} %bitcast.14, ...), custom_call_target="tpu_custom_call" | custom-call | flops 1358954496 | bytes 42467328 | tf_op jit(solution)/shard_map/pallas_call | solution.py:678
  52.9 1.8 %copy.15 = bf16[128,1536]{1,0:T(8,128)(2,1)} copy(bf16[128,1536]{1,0:T(8,128)(2,1)} %shard_map.127) | data formatting | bytes 786432

commit v3 on v2

--- a/solution.py
+++ b/solution.py
@@ -149,6 +149,7 @@
     cum_rows,
     mixed,
     states,
+    nearby,
     chain_out,
     chain_in,
     sums_out,
@@ -282,44 +283,39 @@
             for head in range(first, first + cluster):
                 chain_copy(head).start()
 
+    ready(0, 1, 5, 6, 7)
     causal = row_at >= lane_at
-
-    def attend(i, carry):
-        cols = []
-        for g in range(group):
-            head = i * group + g
-            cols.append(
-                jnp.sum(jnp.where(lane_at == head, padded[...], 0.0), axis=1, keepdims=True)
-            )
+    for head in range(heads):
+        at = slice(head * HEAD, (head + 1) * HEAD)
+        spread = jnp.where(causal, padded[:, head : head + 1] - cum_rows[head : head + 1, :], 0.0)
+        scores = lax.dot_general(
+            query[:, at], key[:, at], (((1,), (1,)), ((), ())), preferred_element_type=F32
+        )
+        weights = jnp.where(causal, scores * jnp.exp(spread), 0.0).astype(BF16)
+        nearby[:, at] = jnp.dot(weights, value[:, at], preferred_element_type=F32)
+
+    def attend(first):
+        these = range(first, first + group)
 
         @pl.when(s > 0)
         def _():
-            for g in range(group):
-                head = i * group + g
+            for head in these:
                 chain_copy(head).wait_recv()
 
                 @pl.when(s < ns - 1)
                 def _():
-                    decay = jnp.exp(cols[g][rows - 1 : rows, :])
+                    decay = jnp.exp(padded[rows - 1 : rows, head : head + 1])
                     prior = chain_in[head].astype(F32)
                     chain_out[head] = (decay * prior + states[head]).astype(BF16)
                     chain_copy(head).start()
 
-        for g in range(group):
-            head = i * group + g
-            at = pl.ds(pl.multiple_of(head * HEAD, HEAD), HEAD)
-            col, row = cols[g], cum_rows[pl.ds(head, 1), :]
-            q, k, v = query[:, at], key[:, at], value[:, at]
-            scores = lax.dot_general(q, k, (((1,), (1,)), ((), ())), preferred_element_type=F32)
-            spread = jnp.where(causal, col - row, 0.0)
-            weights = jnp.where(causal, scores * jnp.exp(spread), 0.0).astype(BF16)
-            nearby = jnp.dot(weights, v, preferred_element_type=F32)
-            inter = jnp.dot(q, chain_in[head], preferred_element_type=F32)
-            attended = nearby + jnp.exp(col) * inter
+        for head in these:
+            at = slice(head * HEAD, (head + 1) * HEAD)
+            inter = jnp.dot(query[:, at], chain_in[head], preferred_element_type=F32)
+            attended = nearby[:, at] + jnp.exp(padded[:, head : head + 1]) * inter
             mean = jnp.sum(attended * attended, axis=1, keepdims=True) / HEAD
-            normed = attended * lax.rsqrt(mean + 1e-06) * attn_gain[pl.ds(head, 1), :]
+            normed = attended * lax.rsqrt(mean + 1e-06) * attn_gain[head : head + 1, :]
             mixed[:, at] = (residual[:, at].astype(F32) + normed).astype(BF16)
-        return carry
 
     def slots_copy(m, a, b):
         return pltpu.make_async_remote_copy(
@@ -341,15 +337,14 @@
             device_id_type=MESH,
         )
 
-    ready(1, 0, 5, 6, 7)
     place_b = place_all.astype(BF16)
-    steps = heads // group // 2
     heads_half = heads // 2
     quarter = half // 2
     logits = jnp.zeros((rows, router.shape[0]), F32)
     squares = jnp.zeros((rows, 1), F32)
     for m in range(2):
-        lax.fori_loop(m * steps, (m + 1) * steps, attend, 0)
+        for first in range(m * heads_half, (m + 1) * heads_half, group):
+            attend(first)
         gained = []
         for head in range(m * heads_half, (m + 1) * heads_half):
             mixed_f = mixed[:, head * HEAD : (head + 1) * HEAD].astype(F32)
@@ -509,26 +504,6 @@
         for a in range(1, ns):
             hidden_copy(p, a).start()
 
-    probs = [jax.nn.sigmoid(added[i : i + 1, :] * inverse) for i in range(2)]
-    gates = [r / (probs[0] + probs[1]) for r in probs]
-    weighted = jnp.concatenate(
-        [
-            place[e]
-            * (
-                jnp.where(id_rows[0] == e, gates[0], 0.0)
-                + jnp.where(id_rows[1] == e, gates[1], 0.0)
-            )
-            for e in range(nx)
-        ],
-        axis=0,
-    )
-    slots = nx * CAP
-    padded[...] = jnp.zeros_like(padded)
-    padded[:slots, :] = weighted
-    weighted = padded[...].T[:, :slots]
-    weighted_high = weighted.astype(BF16)
-    weighted_low = (weighted - weighted_high.astype(F32)).astype(BF16)
-
     def down_product(p, at):
         hidden = jnp.concatenate([hidden_all[i, p] for i in range(ns)], axis=1)
         return jnp.dot(
@@ -585,6 +560,26 @@
         @pl.when(x == s)
         def _():
             back_in[h, x] = back_out[h, s]
+
+    probs = [jax.nn.sigmoid(added[i : i + 1, :] * inverse) for i in range(2)]
+    gates = [r / (probs[0] + probs[1]) for r in probs]
+    weighted = jnp.concatenate(
+        [
+            place[e]
+            * (
+                jnp.where(id_rows[0] == e, gates[0], 0.0)
+                + jnp.where(id_rows[1] == e, gates[1], 0.0)
+            )
+            for e in range(nx)
+        ],
+        axis=0,
+    )
+    slots = nx * CAP
+    padded[...] = jnp.zeros_like(padded)
+    padded[:slots, :] = weighted
+    weighted = padded[...].T[:, :slots]
+    weighted_high = weighted.astype(BF16)
+    weighted_low = (weighted - weighted_high.astype(F32)).astype(BF16)
 
     def out_copy(h):
         at = pl.ds(h * half, half)
@@ -691,6 +686,7 @@
             pltpu.VMEM((rows, rows), F32),
             pltpu.VMEM((rows, width), BF16),
             pltpu.VMEM((heads, HEAD, HEAD), F32),
+            pltpu.VMEM((rows, width), F32),
             pltpu.VMEM((heads, HEAD, HEAD), BF16),
             pltpu.VMEM((heads, HEAD, HEAD), BF16),
             pltpu.VMEM((8, rows), F32),

time: 54.9 us -> 55.4 us (level)
  Pallas kernels: 52.9 us -> 53.5 us
where the time goes in v3:
time: 55.4 us; the launch traced here: 55.3 us
  Pallas kernels  53.5 us (97%)
  local copies, waits for them, and re-layouts  1.77 us (3%)
    pallas_call x1, Pallas kernels, fused_body(): pl.pallas_call(functools.partial(layer_kernel, ns, nx, group, parts), out...  53.5 us
    unnamed x1, local copies, waits for them, and re-layouts  1.77 us

profile of v3, /device:TPU:3, one launch (start us, length us, event | category | flops | bytes accessed | tf_op | source)
XLA Modules:
  0.0 55.3 jit_solution(12372465049120240501)
XLA Ops:
  0.0 53.5 %shard_map.127 = bf16[128,1536]{1,0:T(8,128)(2,1)} custom-call(bf16[128,1536]{1,0:T(8,128)(2,1)} %refs_0_.1, bf16[128,1536]{1,0:T(8,128)(2,1)} %refs_1_.1, bf16[128,1536]{1,0:T(8,128)(2,1)} %refs_2_.1, bf16[128,1536]{1,0:T(8,128)(2,1)} %refs_3_.1, f32[12,128]{1,0:T(8,128)} %bitcast.12, f32[12,128]{1,0:T(8,128)} %bitcast.13, f32[12,128]{1,0:T(8,128)} %bitcast.14, ...), custom_call_target="tpu_custom_call" | custom-call | flops 1358954496 | bytes 42467328 | tf_op jit(solution)/shard_map/pallas_call | solution.py:673
  53.5 1.8 %copy.15 = bf16[128,1536]{1,0:T(8,128)(2,1)} copy(bf16[128,1536]{1,0:T(8,128)(2,1)} %shard_map.127) | data formatting | bytes 786432
